TPU v7x, 512 devices: a whole 4x4x16 slice. The times are simulated.
512 devices in a mesh: section: 2 (over core), row: 16 (over y, x), col: 16 (over z).
Axes of the slice: x: 4, y: 4, z: 16, core: 2. Of those that a mesh axis runs over, the one named last changes fastest.
Arguments:
- features: bfloat16 [2, 64, 128, 2048], P(None, None, 'row', 'col'), may hold values from -6 to 6
- prop_input: bfloat16 [2, 64, 128, 3, 3], P('section'), may hold values from -0.1875 to 0.1875
- prop_middle: bfloat16 [2, 64, 64, 3, 3], P('section'), may hold values from -0.25 to 0.25
- prop_output: bfloat16 [2, 64, 64, 3, 3], P('section'), may hold values from -0.25 to 0.25
- merge_weight: bfloat16 [64, 128, 3, 3], replicated, may hold values from -0.1875 to 0.1875
- first_weight: bfloat16 [64, 64, 3, 3], replicated, may hold values from -0.25 to 0.25
- second_weight: bfloat16 [64, 64, 3, 3], replicated, may hold values from -0.25 to 0.25
- head_weight: bfloat16 [48, 64, 3, 3], replicated, may hold values from -0.25 to 0.25
- cotangent: bfloat16 [2, 3, 512, 8192], P('section', None, 'row', 'col'), may hold values from -6 to 6
Outputs:
- upscaled: float32 [2, 3, 512, 8192], P('section', None, 'row', 'col')
- adjoint: float32 [2, 128, 128, 2048], P('section', None, 'row', 'col')
All inputs are finite; a program needn't handle non-finite values.
Results may differ from a plain program's by a relative error of at most 0.015.
Values may be sent and summed in bfloat16 or wider, within the bound.
A program may use at most 64 MiB of HBM per device.

v0:
```python
import functools

import jax
import jax.numpy as jnp
from jax import lax
from jax.experimental import pallas as pl
from jax.experimental.pallas import tpu as pltpu
from jax.sharding import PartitionSpec as P

F32 = jnp.float32
BF16 = jnp.bfloat16
MESH = pl.DeviceIdType.MESH

RIM = 16
COLS = 128
WIDE = COLS + 2 * RIM
OWN = 4
PAIR = 128

AROUND = tuple((dr, dc) for dr in (-1, 0, 1) for dc in (-1, 0, 1) if (dr, dc) != (0, 0))

EX_FIRST, EX_SECOND, EX_COT, EX_STATE1, EX_STATE2 = range(5)


def iota(shape, dim):
    return lax.broadcasted_iota(jnp.int32, shape, dim)


def one_hot(cond):
    return jnp.where(cond, 1.0, 0.0).astype(F32)


def low_lanes(shape):
    return iota(shape, len(shape) - 1) < 64


def kernel(
    rows,
    cols,
    feat,
    w_input,
    w_middle,
    w_output,
    w_merge,
    w_first,
    w_second,
    w_head,
    cot,
    up_out,
    adj_out,
    feat_v,
    w_input_v,
    w_middle_v,
    w_output_v,
    w_merge_v,
    w_first_v,
    w_second_v,
    w_head_v,
    cot_v,
    stage,
    xf1,
    xf2,
    xo2,
    cb,
    s1,
    s2,
    e1,
    lift1,
    inner1,
    state1,
    lift2,
    inner2,
    merged,
    slope_m,
    rec_inner,
    refined,
    grad_ref,
    grad_in_pre,
    grad_in,
    grad_pre,
    k_feat,
    k_state,
    k_middle,
    k_output,
    k_merge2,
    k_merge1,
    k_first,
    k_second,
    k_head,
    k_head_t,
    k_second_t,
    k_first_t,
    k_merge_t,
    head_rows,
    shuffle,
    z_hi,
    z_lo,
    up_v,
    adj_v,
    col_mask,
    load_sem,
    store_sem,
    send_sem,
    recv_sem,
):
    sec = lax.axis_index("section")
    row = lax.axis_index("row")
    col = lax.axis_index("col")
    other = 1 - sec
    first_frame = 1 - sec
    second_frame = sec

    loads = []

    def load(source, target):
        copy = pltpu.make_async_copy(source, target, load_sem.at[len(loads)])
        copy.start()
        loads.append(copy)
        return copy

    load_f1 = load(feat.at[first_frame], feat_v.at[0])
    load_f2 = load(feat.at[second_frame], feat_v.at[1])
    load_cot = load(cot, cot_v)
    load_prop = [load(w_input, w_input_v), load(w_middle, w_middle_v), load(w_output, w_output_v)]
    load_head = load(w_head, w_head_v)
    load_second = load(w_second, w_second_v)
    load_merge = load(w_merge, w_merge_v)
    load_first = load(w_first, w_first_v)

    barrier = pltpu.get_barrier_semaphore()

    def place(dr, dc, section):
        return (section, lax.rem(row + dr + rows, rows), lax.rem(col + dc + cols, cols))

    partners = [place(dr, dc, s) for dr, dc in AROUND for s in (sec, other)] + [(other, row, col)]
    for partner in partners:
        pl.semaphore_signal(barrier, inc=1, device_id=partner, device_id_type=MESH)

    def exchange(kind, src, src_pair, src_col, dst, halo, section):
        copies = []
        for k, (dr, dc) in enumerate(AROUND):
            sp, n, dp = {-1: (0, halo, halo + OWN), 0: (0, OWN, halo), 1: (OWN - halo, halo, 0)}[dr]
            sc, m, dcol = {
                -1: (0, RIM, RIM + COLS),
                0: (0, COLS, RIM),
                1: (COLS - RIM, RIM, 0),
            }[dc]
            copies.append(
                pltpu.make_async_remote_copy(
                    src_ref=src.at[pl.ds(src_pair + sp, n), pl.ds(src_col + sc, m), :],
                    dst_ref=dst.at[pl.ds(dp, n), pl.ds(dcol, m), :],
                    send_sem=send_sem.at[kind, k],
                    recv_sem=recv_sem.at[kind, k],
                    device_id=place(dr, dc, section),
                    device_id_type=MESH,
                )
            )
        return copies

    def clear_outside(buf, halo):
        pairs = buf.shape[0]

        @pl.when(row == 0)
        def _():
            buf[pl.ds(0, halo)] = jnp.zeros((halo, WIDE, PAIR), BF16)

        @pl.when(row == rows - 1)
        def _():
            buf[pl.ds(halo + OWN, halo)] = jnp.zeros((halo, WIDE, PAIR), BF16)

        @pl.when(col == 0)
        def _():
            buf[:, pl.ds(0, RIM), :] = jnp.zeros((pairs, RIM, PAIR), BF16)

        @pl.when(col == cols - 1)
        def _():
            buf[:, pl.ds(RIM + COLS, RIM), :] = jnp.zeros((pairs, RIM, PAIR), BF16)

    def turn_features(at, dst, halo):
        stage[...] = feat_v[at].astype(F32)
        for p in range(OWN):
            two = jnp.concatenate(
                [stage[pl.ds(2 * p + r, 64, stride=8), :] for r in range(2)], axis=0
            )
            dst[halo + p, pl.ds(RIM, COLS), :] = two.T.astype(BF16)

    load_f1.wait()
    turn_features(0, xf1, 3)
    pl.semaphore_wait(barrier, len(partners))
    ex_first = exchange(EX_FIRST, xf1, 3, RIM, xf1, 3, sec)
    for copy in ex_first:
        copy.start()
    load_f2.wait()
    turn_features(1, xf2, 2)
    ex_second = exchange(EX_SECOND, xf2, 2, RIM, xf2, 2, sec)
    for copy in ex_second:
        copy.start()

    k_at, n_at = iota((512, 512), 0), iota((512, 512), 1)
    shuffle[...] = one_hot(n_at == 4 * (k_at & 127) + (k_at >> 7)).astype(BF16)
    m_at, n_at = iota((128, 96), 0), iota((128, 96), 1)
    spread = one_hot(
        (((n_at >> 2) & 7) == (m_at >> 4)) & (((n_at >> 5) * 4 + (n_at & 3)) == (m_at & 15))
    ).astype(BF16)
    load_cot.wait()
    spaced = jnp.dot(spread, cot_v[...], preferred_element_type=F32).astype(BF16)
    parted = lax.dot_general(
        spaced, shuffle[...], (((1,), (1,)), ((), ())), preferred_element_type=F32
    )
    for p in range(OWN):
        pieces = [
            parted[(2 * p + r) * 16 : (2 * p + r + 1) * 16, j * 128 : (j + 1) * 128]
            for r in range(2)
            for j in range(4)
        ]
        cb[2 + p, pl.ds(RIM, COLS), :] = jnp.concatenate(pieces, axis=0).T.astype(BF16)
    ex_cot = exchange(EX_COT, cb, 2, RIM, cb, 2, sec)
    for copy in ex_cot:
        copy.start()

    col_at = iota((WIDE, PAIR), 0) - RIM + col * COLS
    col_mask[...] = one_hot((col_at >= 0) & (col_at < cols * COLS))

    def pack_forward(tap, targets):
        empty = jnp.zeros(tap(0, 0).shape, F32)
        for b in range(3):
            for q in range(4):
                upper = tap(q, b) if q < 3 else empty
                lower = tap(q - 1, b) if q > 0 else empty
                turned = jnp.concatenate([upper, lower], axis=0).T.astype(BF16)
                for t, target in enumerate(targets):
                    target[q * 64 : (q + 1) * 64, b * 128 : (b + 1) * 128] = turned[
                        t * 64 : (t + 1) * 64
                    ]

    def pack_transposed(tap, target):
        width = tap(0, 0).shape[1]
        empty = jnp.zeros((64, width), F32)
        for b in range(3):
            for q in range(4):
                left = tap(q, b) if q < 3 else empty
                right = tap(q - 1, b) if q > 0 else empty
                target[q * 64 : (q + 1) * 64, b * 2 * width : (b + 1) * 2 * width] = (
                    jnp.concatenate([left, right], axis=1).astype(BF16)
                )

    for copy in load_prop:
        copy.wait()
    pack_forward(lambda a, b: w_input_v[a, b].astype(F32), (k_feat, k_state))
    pack_forward(lambda a, b: w_middle_v[a, b].astype(F32), (k_middle,))
    pack_forward(lambda a, b: w_output_v[a, b].astype(F32), (k_output,))

    def conv(sources, matrices, j):
        total = None
        for source, matrix in zip(sources, matrices):
            x = jnp.concatenate([source[j], source[j + 1]], axis=1)
            y = jnp.dot(x, matrix[...], preferred_element_type=F32)
            total = y if total is None else total + y
        w = total.shape[1] // 3
        return (
            total[:, w : 2 * w]
            + pltpu.roll(total[:, :w], 1, 0)
            + pltpu.roll(total[:, 2 * w :], WIDE - 1, 0)
        )

    def inside(start):
        at = row * (2 * OWN) + start + jnp.where(low_lanes((1, PAIR)), 0, 1)
        return col_mask[...] * one_hot((at >= 0) & (at < rows * 2 * OWN))

    def lrelu(v):
        return jnp.where(v > 0, v, 0.1 * v)

    def realign(upper_of, lower_of):
        mixed = jnp.where(
            low_lanes(upper_of.shape), lower_of.astype(F32), upper_of.astype(F32)
        )
        return pltpu.roll(mixed, 64, 1).astype(BF16)

    for copy in ex_first:
        copy.wait_recv()
    clear_outside(xf1, 3)
    for j in range(9):
        v = conv((xf1,), (k_feat,), j)
        lift1[j] = (lrelu(v) * inside(2 * j - 5)).astype(BF16)
    for j in range(8):
        v = conv((lift1,), (k_middle,), j)
        inner1[j] = (jnp.maximum(v, 0.0) * inside(2 * j - 4)).astype(BF16)
    for j in range(7):
        v = conv((inner1,), (k_output,), j) + lift1[j + 1].astype(F32)
        state1[j] = (v * inside(2 * j - 3)).astype(BF16)
    for p in range(OWN):
        e1[p] = realign(
            state1[p + 1, pl.ds(RIM, COLS), :], state1[p + 2, pl.ds(RIM, COLS), :]
        )
    ex_state1 = exchange(EX_STATE1, e1, 0, 0, s1, 2, other)
    ex_state1.append(
        pltpu.make_async_remote_copy(
            src_ref=e1,
            dst_ref=s1.at[pl.ds(2, OWN), pl.ds(RIM, COLS), :],
            send_sem=send_sem.at[EX_STATE1, 8],
            recv_sem=recv_sem.at[EX_STATE1, 8],
            device_id=(other, row, col),
            device_id_type=MESH,
        )
    )
    for copy in ex_state1:
        copy.start()

    for copy in ex_second:
        copy.wait_recv()
    clear_outside(xf2, 2)
    for j in range(7):
        xo2[j] = realign(xf2[j], xf2[j + 1])
    for j in range(6):
        v = conv((xo2, state1), (k_feat, k_state), j)
        lift2[j] = (lrelu(v) * inside(2 * j - 2)).astype(BF16)
    for j in range(5):
        v = conv((lift2,), (k_middle,), j)
        inner2[j] = (jnp.maximum(v, 0.0) * inside(2 * j - 1)).astype(BF16)
    for j in range(4):
        v = conv((inner2,), (k_output,), j) + lift2[j + 1].astype(F32)
        s2[2 + j, pl.ds(RIM, COLS), :] = v[RIM : RIM + COLS].astype(BF16)
    ex_state2 = exchange(EX_STATE2, s2, 2, RIM, s2, 2, sec)
    for copy in ex_state2:
        copy.start()

    load_head.wait()
    m_at, n_at = iota((64, 48), 0), iota((64, 48), 1)
    order = one_hot((n_at == (m_at & 15) * 4 + (m_at >> 4)) & ((m_at & 15) < 12)).astype(BF16)
    for a in range(3):
        for b in range(3):
            head_rows[a, b] = jnp.dot(order, w_head_v[a, b], preferred_element_type=F32)
    pack_transposed(lambda a, b: head_rows[2 - a, 2 - b], k_head_t)
    load_second.wait()
    pack_transposed(lambda a, b: w_second_v[2 - a, 2 - b].astype(F32), k_second_t)

    for copy in ex_cot:
        copy.wait_recv()
    clear_outside(cb, 2)
    for j in range(7):
        v = conv((cb,), (k_head_t,), j)
        grad_ref[j] = (v * inside(2 * j - 3)).astype(BF16)
    for j in range(6):
        grad_in_pre[j] = conv((grad_ref,), (k_second_t,), j) * inside(2 * j - 2)

    load_merge.wait()

    @pl.when(sec == 0)
    def _():
        pack_forward(lambda a, b: w_merge_v[a, b].astype(F32), (k_merge2, k_merge1))

    @pl.when(sec == 1)
    def _():
        pack_forward(lambda a, b: w_merge_v[a, b].astype(F32), (k_merge1, k_merge2))

    load_first.wait()
    pack_forward(lambda a, b: w_first_v[a, b].astype(F32), (k_first,))
    pack_forward(lambda a, b: w_second_v[a, b].astype(F32), (k_second,))
    pack_forward(lambda a, b: head_rows[a, b], (k_head,))
    pack_transposed(lambda a, b: w_first_v[2 - a, 2 - b].astype(F32), k_first_t)
    pack_transposed(lambda a, b: w_merge_v[2 - a, 2 - b].astype(F32), k_merge_t)

    for copy in ex_state1:
        copy.wait_recv()
    clear_outside(s1, 2)
    for copy in ex_state2:
        copy.wait_recv()
    clear_outside(s2, 2)
    for j in range(7):
        v = conv((s1, s2), (k_merge1, k_merge2), j)
        sigma = jax.nn.sigmoid(v)
        merged[j] = (v * sigma * inside(2 * j - 3)).astype(BF16)
        if 1 <= j <= 5:
            slope_m[j - 1] = sigma * (1.0 + v * (1.0 - sigma)) * inside(2 * j - 3)
    for j in range(6):
        v = conv((merged,), (k_first,), j)
        sigma = jax.nn.sigmoid(v)
        rec_inner[j] = (v * sigma * inside(2 * j - 2)).astype(BF16)
        grad_in[j] = (grad_in_pre[j] * (sigma * (1.0 + v * (1.0 - sigma)))).astype(BF16)
    for j in range(5):
        v = conv((rec_inner,), (k_second,), j) + merged[j + 1].astype(F32)
        refined[j] = (v * inside(2 * j - 1)).astype(BF16)
    for j in range(4):
        v = conv((refined,), (k_head,), j)[RIM : RIM + COLS].T
        high = v.astype(BF16)
        low = (v - high.astype(F32)).astype(BF16)
        for r in range(2):
            for i in range(4):
                piece = slice((r * 4 + i) * 16, (r * 4 + i + 1) * 16)
                at = (slice((2 * j + r) * 16, (2 * j + r + 1) * 16), slice(i * 128, (i + 1) * 128))
                z_hi[at] = high[piece]
                z_lo[at] = low[piece]
    m_at, n_at = iota((96, 128), 0), iota((96, 128), 1)
    gather = one_hot(
        (((m_at >> 2) & 7) == (n_at >> 4)) & (((m_at >> 5) * 4 + (m_at & 3)) == (n_at & 15))
    ).astype(BF16)
    total = None
    for z in (z_hi, z_lo):
        ordered = jnp.dot(gather, z[...], preferred_element_type=F32).astype(BF16)
        part = jnp.dot(ordered, shuffle[...], preferred_element_type=F32)
        total = part if total is None else total + part
    up_v[...] = total
    store_up = pltpu.make_async_copy(up_v, up_out, store_sem.at[0])
    store_up.start()

    for j in range(5):
        v = conv((grad_in,), (k_first_t,), j) + grad_ref[j + 1].astype(F32)
        grad_pre[j] = (v * slope_m[j]).astype(BF16)
    for j in range(4):
        v = conv((grad_pre,), (k_merge_t,), j)
        for r in range(2):
            adj_v[pl.ds(2 * j + r, 128, stride=8), :] = v[
                RIM : RIM + COLS, r * 128 : (r + 1) * 128
            ].T
    store_adj = pltpu.make_async_copy(adj_v, adj_out, store_sem.at[1])
    store_adj.start()

    for copies in (ex_first, ex_second, ex_cot, ex_state1, ex_state2):
        for copy in copies:
            copy.wait_send()
    store_up.wait()
    store_adj.wait()


def on_device(
    rows,
    cols,
    features,
    prop_input,
    prop_middle,
    prop_output,
    merge_weight,
    first_weight,
    second_weight,
    head_weight,
    cotangent,
):
    def taps(weight):
        return jnp.transpose(weight, (2, 3, 0, 1))

    def vmem(*shape, dtype=BF16):
        return pltpu.VMEM(shape, dtype)

    def act(pairs, dtype=BF16):
        return pltpu.VMEM((pairs, WIDE, PAIR), dtype)

    scratch = (
        [
            vmem(2, 512, 128),
            vmem(3, 3, 64, 128),
            vmem(3, 3, 64, 64),
            vmem(3, 3, 64, 64),
            vmem(3, 3, 64, 128),
            vmem(3, 3, 64, 64),
            vmem(3, 3, 64, 64),
            vmem(3, 3, 48, 64),
            vmem(96, 512),
            vmem(512, 128, dtype=F32),
            act(10),
            act(8),
            act(7),
            act(8),
            act(8),
            act(8),
            vmem(OWN, COLS, PAIR),
            act(9),
            act(8),
            act(7),
            act(6),
            act(5),
            act(7),
            act(5, F32),
            act(6),
            act(5),
            act(7),
            act(6, F32),
            act(6),
            act(5),
        ]
        + [vmem(256, 384) for _ in range(12)]
        + [
            vmem(256, 768),
            vmem(3, 3, 64, 64, dtype=F32),
            vmem(512, 512),
            vmem(128, 512),
            vmem(128, 512),
            vmem(96, 512, dtype=F32),
            vmem(1024, 128, dtype=F32),
            vmem(WIDE, PAIR, dtype=F32),
            pltpu.SemaphoreType.DMA((10,)),
            pltpu.SemaphoreType.DMA((2,)),
            pltpu.SemaphoreType.DMA((5, 9)),
            pltpu.SemaphoreType.DMA((5, 9)),
        ]
    )
    up, adj = pl.pallas_call(
        functools.partial(kernel, rows, cols),
        out_shape=(
            jax.ShapeDtypeStruct((96, 512), F32),
            jax.ShapeDtypeStruct((1024, 128), F32),
        ),
        in_specs=[pl.BlockSpec(memory_space=pl.ANY)] * 9,
        out_specs=(pl.BlockSpec(memory_space=pl.ANY), pl.BlockSpec(memory_space=pl.ANY)),
        scratch_shapes=scratch,
        compiler_params=pltpu.CompilerParams(
            collective_id=0, has_side_effects=True, vmem_limit_bytes=48 * 1024 * 1024
        ),
    )(
        features.reshape(2, 512, 128),
        taps(prop_input[0]),
        taps(prop_middle[0]),
        taps(prop_output[0]),
        taps(merge_weight),
        taps(first_weight),
        taps(second_weight),
        taps(head_weight),
        cotangent.reshape(96, 512),
    )
    return up.reshape(1, 3, 32, 512), adj.reshape(1, 128, 8, 128)


def solution(mesh):
    rows, cols = mesh.shape["row"], mesh.shape["col"]
    placed = (
        P(None, None, "row", "col"),
        P("section", None, None, None, None),
        P("section", None, None, None, None),
        P("section", None, None, None, None),
        P(),
        P(),
        P(),
        P(),
        P("section", None, "row", "col"),
    )
    return jax.shard_map(
        functools.partial(on_device, rows, cols),
        mesh=mesh,
        in_specs=placed,
        out_specs=(P("section", None, "row", "col"), P("section", None, "row", "col")),
        check_vma=False,
    )
```

profile of v0, /device:TPU:1, one launch (start us, length us, event | category | flops | bytes accessed | tf_op | source)
XLA Modules:
  0.0 45.8 jit_solution(10227135983383681935)
XLA Ops:
  0.6 0.0 copy-start
  0.6 0.9 %copy-done = bf16[2,64,8,128]{3,2,1,0:T(8,128)(2,1)S(1)} copy-done((bf16[2,64,8,128]{3,2,1,0:T(8,128)(2,1)S(1)}, bf16[2,64,8,128]{3,2,1,0:T(8,128)(2,1)}, u32[]{:S(2)}) %copy-start) | copy-done | bytes 262168
  1.6 0.0 copy-start.1
  1.6 0.9 %copy-done.1 = bf16[1,64,128,3,3]{2,1,4,3,0:T(8,128)(2,1)S(1)} copy-done((bf16[1,64,128,3,3]{2,1,4,3,0:T(8,128)(2,1)S(1)}, bf16[1,64,128,3,3]{2,1,4,3,0:T(8,128)(2,1)}, u32[]{:S(2)}) %copy-start.1) | copy-done | bytes 147480
  2.5 0.0 copy-start.2
  2.5 0.9 %copy-done.2 = bf16[1,64,64,3,3]{2,1,4,3,0:T(8,128)(2,1)S(1)} copy-done((bf16[1,64,64,3,3]{2,1,4,3,0:T(8,128)(2,1)S(1)}, bf16[1,64,64,3,3]{2,1,4,3,0:T(8,128)(2,1)}, u32[]{:S(2)}) %copy-start.2) | copy-done | bytes 73752
  3.4 0.0 copy-start.3
  3.4 0.9 %copy-done.3 = bf16[1,64,64,3,3]{2,1,4,3,0:T(8,128)(2,1)S(1)} copy-done((bf16[1,64,64,3,3]{2,1,4,3,0:T(8,128)(2,1)S(1)}, bf16[1,64,64,3,3]{2,1,4,3,0:T(8,128)(2,1)}, u32[]{:S(2)}) %copy-start.3) | copy-done | bytes 73752
  4.3 0.0 copy-start.4
  4.3 0.9 %copy-done.4 = bf16[64,128,3,3]{1,0,3,2:T(8,128)(2,1)S(1)} copy-done((bf16[64,128,3,3]{1,0,3,2:T(8,128)(2,1)S(1)}, bf16[64,128,3,3]{1,0,3,2:T(8,128)(2,1)}, u32[]{:S(2)}) %copy-start.4) | copy-done | bytes 147480
  5.2 0.0 copy-start.5
  5.2 0.9 %copy-done.5 = bf16[64,64,3,3]{1,0,3,2:T(8,128)(2,1)S(1)} copy-done((bf16[64,64,3,3]{1,0,3,2:T(8,128)(2,1)S(1)}, bf16[64,64,3,3]{1,0,3,2:T(8,128)(2,1)}, u32[]{:S(2)}) %copy-start.5) | copy-done | bytes 73752
  6.1 0.0 copy-start.6
  6.1 0.9 %copy-done.6 = bf16[64,64,3,3]{1,0,3,2:T(8,128)(2,1)S(1)} copy-done((bf16[64,64,3,3]{1,0,3,2:T(8,128)(2,1)S(1)}, bf16[64,64,3,3]{1,0,3,2:T(8,128)(2,1)}, u32[]{:S(2)}) %copy-start.6) | copy-done | bytes 73752
  7.0 0.0 copy-start.7
  7.0 0.9 %copy-done.7 = bf16[48,64,3,3]{1,0,3,2:T(8,128)(2,1)S(1)} copy-done((bf16[48,64,3,3]{1,0,3,2:T(8,128)(2,1)S(1)}, bf16[48,64,3,3]{1,0,3,2:T(8,128)(2,1)}, u32[]{:S(2)}) %copy-start.7) | copy-done | bytes 55320
  7.9 0.0 copy-start.8
  7.9 0.9 %copy-done.8 = bf16[1,3,32,512]{3,2,1,0:T(8,128)(2,1)S(1)} copy-done((bf16[1,3,32,512]{3,2,1,0:T(8,128)(2,1)S(1)}, bf16[1,3,32,512]{3,2,1,0:T(8,128)(2,1)}, u32[]{:S(2)}) %copy-start.8) | copy-done | bytes 98328
  8.8 35.5 %shard_map.104 = (f32[96,512]{1,0:T(8,128)S(1)}, f32[1024,128]{1,0:T(8,128)S(1)}) custom-call(bf16[2,512,128]{2,1,0:T(8,128)(2,1)S(1)} %bitcast.18, bf16[3,3,64,128]{3,2,1,0:T(8,128)(2,1)S(1)} %bitcast.20, bf16[3,3,64,64]{3,2,1,0:T(8,128)(2,1)S(1)} %bitcast.21, bf16[3,3,64,64]{3,2,1,0:T(8,128)(2,1)S(1)} %bitcast.22, bf16[3,3,64,128]{3,2,1,0:T(8,128)(2,1)S(1)} %bitcast.23, ...), custom_call_target="tpu_custom_call" | custom-call | tf_op jit(solution)/shard_map/pallas_call | solution.py:496
  44.3 0.7 %copy.13 = f32[1,3,32,512]{3,2,1,0:T(8,128)} copy(f32[1,3,32,512]{3,2,1,0:T(8,128)S(1)} %bitcast.19) | data formatting | bytes 393216
  45.0 0.8 %copy.14 = f32[1,128,8,128]{3,2,1,0:T(8,128)} copy(f32[1,128,8,128]{3,2,1,0:T(8,128)S(1)} %bitcast.17) | data formatting | bytes 1048576
Async XLA Ops:
  0.6 1.0 %copy-start = (bf16[2,64,8,128]{3,2,1,0:T(8,128)(2,1)S(1)}, bf16[2,64,8,128]{3,2,1,0:T(8,128)(2,1)}, u32[]{:S(2)}) copy-start(bf16[2,64,8,128]{3,2,1,0:T(8,128)(2,1)} %param.9) | copy-start | bytes 786436
  1.6 0.9 %copy-start.1 = (bf16[1,64,128,3,3]{2,1,4,3,0:T(8,128)(2,1)S(1)}, bf16[1,64,128,3,3]{2,1,4,3,0:T(8,128)(2,1)}, u32[]{:S(2)}) copy-start(bf16[1,64,128,3,3]{2,1,4,3,0:T(8,128)(2,1)} %param.10) | copy-start | bytes 442372
  2.5 0.9 %copy-start.2 = (bf16[1,64,64,3,3]{2,1,4,3,0:T(8,128)(2,1)S(1)}, bf16[1,64,64,3,3]{2,1,4,3,0:T(8,128)(2,1)}, u32[]{:S(2)}) copy-start(bf16[1,64,64,3,3]{2,1,4,3,0:T(8,128)(2,1)} %param.11) | copy-start | bytes 221188
  3.4 0.9 %copy-start.3 = (bf16[1,64,64,3,3]{2,1,4,3,0:T(8,128)(2,1)S(1)}, bf16[1,64,64,3,3]{2,1,4,3,0:T(8,128)(2,1)}, u32[]{:S(2)}) copy-start(bf16[1,64,64,3,3]{2,1,4,3,0:T(8,128)(2,1)} %param.12) | copy-start | bytes 221188
  4.3 0.9 %copy-start.4 = (bf16[64,128,3,3]{1,0,3,2:T(8,128)(2,1)S(1)}, bf16[64,128,3,3]{1,0,3,2:T(8,128)(2,1)}, u32[]{:S(2)}) copy-start(bf16[64,128,3,3]{1,0,3,2:T(8,128)(2,1)} %param.13) | copy-start | bytes 442372
  5.2 0.9 %copy-start.5 = (bf16[64,64,3,3]{1,0,3,2:T(8,128)(2,1)S(1)}, bf16[64,64,3,3]{1,0,3,2:T(8,128)(2,1)}, u32[]{:S(2)}) copy-start(bf16[64,64,3,3]{1,0,3,2:T(8,128)(2,1)} %param.14) | copy-start | bytes 221188
  6.1 0.9 %copy-start.6 = (bf16[64,64,3,3]{1,0,3,2:T(8,128)(2,1)S(1)}, bf16[64,64,3,3]{1,0,3,2:T(8,128)(2,1)}, u32[]{:S(2)}) copy-start(bf16[64,64,3,3]{1,0,3,2:T(8,128)(2,1)} %param.15) | copy-start | bytes 221188
  7.0 0.9 %copy-start.7 = (bf16[48,64,3,3]{1,0,3,2:T(8,128)(2,1)S(1)}, bf16[48,64,3,3]{1,0,3,2:T(8,128)(2,1)}, u32[]{:S(2)}) copy-start(bf16[48,64,3,3]{1,0,3,2:T(8,128)(2,1)} %param.16) | copy-start | bytes 165892
  7.9 0.9 %copy-start.8 = (bf16[1,3,32,512]{3,2,1,0:T(8,128)(2,1)S(1)}, bf16[1,3,32,512]{3,2,1,0:T(8,128)(2,1)}, u32[]{:S(2)}) copy-start(bf16[1,3,32,512]{3,2,1,0:T(8,128)(2,1)} %param.17) | copy-start | bytes 294916
where the time goes:
time: 46.1 us; the launch traced here: 45.8 us
  Pallas kernels  35.5 us (77%)
  local copies, waits for them, and re-layouts  9.66 us (21%)
  between operations  0.66 us (1%)
    pallas_call x1, Pallas kernels, on_device(): pl.pallas_call(functools.partial(kernel, rows, cols), out_shape=(jax.Shap...  35.5 us
    unnamed x20, local copies, waits for them, and re-layouts  9.66 us

commit v1 on v0

--- a/solution.py
+++ b/solution.py
@@ -17,9 +17,14 @@
 OWN = 4
 PAIR = 128
 
-AROUND = tuple((dr, dc) for dr in (-1, 0, 1) for dc in (-1, 0, 1) if (dr, dc) != (0, 0))
-
-EX_FIRST, EX_SECOND, EX_COT, EX_STATE1, EX_STATE2 = range(5)
+HALO_A, HALO_B, HALO_C = 5, 4, 2
+REACH = 2
+
+AROUND = tuple(
+    (dr, dc) for dr in (-1, 1, 0, -2, 2) for dc in (0, -1, 1) if (dr, dc) != (0, 0)
+)
+
+EX_FIRST, EX_SECOND, EX_COT, EX_KERNELS = range(4)
 
 
 def iota(shape, dim):
@@ -64,12 +69,13 @@
     cb,
     s1,
     s2,
-    e1,
     lift1,
     inner1,
     state1,
     lift2,
     inner2,
+    lift3,
+    inner3,
     merged,
     slope_m,
     rec_inner,
@@ -82,6 +88,9 @@
     k_state,
     k_middle,
     k_output,
+    k_feat_o,
+    k_middle_o,
+    k_output_o,
     k_merge2,
     k_merge1,
     k_first,
@@ -129,52 +138,85 @@
 
     barrier = pltpu.get_barrier_semaphore()
 
-    def place(dr, dc, section):
-        return (section, lax.rem(row + dr + rows, rows), lax.rem(col + dc + cols, cols))
-
-    partners = [place(dr, dc, s) for dr, dc in AROUND for s in (sec, other)] + [(other, row, col)]
-    for partner in partners:
-        pl.semaphore_signal(barrier, inc=1, device_id=partner, device_id_type=MESH)
-
-    def exchange(kind, src, src_pair, src_col, dst, halo, section):
+    def exists(dr, dc):
+        there = None
+        for at, size, d in ((row, rows, dr), (col, cols, dc)):
+            if d != 0:
+                ok = at + d < size if d > 0 else at + d >= 0
+                there = ok if there is None else there & ok
+        return there
+
+    def place(dr, dc):
+        return (sec, lax.rem(row + dr + rows, rows), lax.rem(col + dc + cols, cols))
+
+    for dr, dc in AROUND:
+
+        @pl.when(exists(dr, dc))
+        def _(dr=dr, dc=dc):
+            pl.semaphore_signal(barrier, inc=1, device_id=place(dr, dc), device_id_type=MESH)
+
+    @pl.when(sec == 1)
+    def _():
+        pl.semaphore_signal(barrier, inc=1, device_id=(other, row, col), device_id_type=MESH)
+
+    near_rows = jnp.minimum(row + REACH, rows - 1) - jnp.maximum(row - REACH, 0) + 1
+    near_cols = jnp.minimum(col + 1, cols - 1) - jnp.maximum(col - 1, 0) + 1
+    greetings = near_rows * near_cols - sec
+
+    def exchange(kind, buf, halo):
         copies = []
         for k, (dr, dc) in enumerate(AROUND):
-            sp, n, dp = {-1: (0, halo, halo + OWN), 0: (0, OWN, halo), 1: (OWN - halo, halo, 0)}[dr]
+            if abs(dr) == 2 and halo <= OWN:
+                continue
+            n = {0: OWN, 1: min(halo, OWN), 2: halo - OWN}[abs(dr)]
+            sp = OWN - n if dr > 0 else 0
+            dp = halo + sp - OWN * dr
             sc, m, dcol = {
                 -1: (0, RIM, RIM + COLS),
                 0: (0, COLS, RIM),
                 1: (COLS - RIM, RIM, 0),
             }[dc]
-            copies.append(
-                pltpu.make_async_remote_copy(
-                    src_ref=src.at[pl.ds(src_pair + sp, n), pl.ds(src_col + sc, m), :],
-                    dst_ref=dst.at[pl.ds(dp, n), pl.ds(dcol, m), :],
-                    send_sem=send_sem.at[kind, k],
-                    recv_sem=recv_sem.at[kind, k],
-                    device_id=place(dr, dc, section),
-                    device_id_type=MESH,
-                )
+            copy = pltpu.make_async_remote_copy(
+                src_ref=buf.at[pl.ds(halo + sp, n), pl.ds(RIM + sc, m), :],
+                dst_ref=buf.at[pl.ds(dp, n), pl.ds(dcol, m), :],
+                send_sem=send_sem.at[kind, k],
+                recv_sem=recv_sem.at[kind, k],
+                device_id=place(dr, dc),
+                device_id_type=MESH,
             )
+            copies.append((copy, exists(dr, dc), exists(-dr, -dc)))
         return copies
 
-    def clear_outside(buf, halo):
-        pairs = buf.shape[0]
-
-        @pl.when(row == 0)
-        def _():
-            buf[pl.ds(0, halo)] = jnp.zeros((halo, WIDE, PAIR), BF16)
-
-        @pl.when(row == rows - 1)
-        def _():
-            buf[pl.ds(halo + OWN, halo)] = jnp.zeros((halo, WIDE, PAIR), BF16)
-
-        @pl.when(col == 0)
-        def _():
-            buf[:, pl.ds(0, RIM), :] = jnp.zeros((pairs, RIM, PAIR), BF16)
-
-        @pl.when(col == cols - 1)
-        def _():
-            buf[:, pl.ds(RIM + COLS, RIM), :] = jnp.zeros((pairs, RIM, PAIR), BF16)
+    def start_all(copies):
+        for copy, to, _ in copies:
+            pl.when(to)(copy.start)
+
+    def receive_all(copies):
+        for copy, _, source in copies:
+            pl.when(source)(copy.wait_recv)
+
+    def sent_all(copies):
+        for copy, to, _ in copies:
+            pl.when(to)(copy.wait_send)
+
+    halos = ((xf1, HALO_A), (xf2, HALO_B), (cb, HALO_C))
+
+    def clear_rows(up, tiles):
+        for buf, halo in halos:
+            n = halo - OWN * tiles
+            if n > 0:
+                at = 0 if up else buf.shape[0] - n
+                buf[pl.ds(at, n)] = jnp.zeros((n, WIDE, PAIR), BF16)
+
+    def clear_cols(at):
+        for buf, _ in halos:
+            buf[:, pl.ds(at, RIM), :] = jnp.zeros((buf.shape[0], RIM, PAIR), BF16)
+
+    for tiles in range(REACH):
+        pl.when(row == tiles)(functools.partial(clear_rows, True, tiles))
+        pl.when(row == rows - 1 - tiles)(functools.partial(clear_rows, False, tiles))
+    pl.when(col == 0)(functools.partial(clear_cols, 0))
+    pl.when(col == cols - 1)(functools.partial(clear_cols, RIM + COLS))
 
     def turn_features(at, dst, halo):
         stage[...] = feat_v[at].astype(F32)
@@ -185,16 +227,14 @@
             dst[halo + p, pl.ds(RIM, COLS), :] = two.T.astype(BF16)
 
     load_f1.wait()
-    turn_features(0, xf1, 3)
-    pl.semaphore_wait(barrier, len(partners))
-    ex_first = exchange(EX_FIRST, xf1, 3, RIM, xf1, 3, sec)
-    for copy in ex_first:
-        copy.start()
+    turn_features(0, xf1, HALO_A)
+    pl.semaphore_wait(barrier, greetings)
+    ex_first = exchange(EX_FIRST, xf1, HALO_A)
+    start_all(ex_first)
     load_f2.wait()
-    turn_features(1, xf2, 2)
-    ex_second = exchange(EX_SECOND, xf2, 2, RIM, xf2, 2, sec)
-    for copy in ex_second:
-        copy.start()
+    turn_features(1, xf2, HALO_B)
+    ex_second = exchange(EX_SECOND, xf2, HALO_B)
+    start_all(ex_second)
 
     k_at, n_at = iota((512, 512), 0), iota((512, 512), 1)
     shuffle[...] = one_hot(n_at == 4 * (k_at & 127) + (k_at >> 7)).astype(BF16)
@@ -213,10 +253,9 @@
             for r in range(2)
             for j in range(4)
         ]
-        cb[2 + p, pl.ds(RIM, COLS), :] = jnp.concatenate(pieces, axis=0).T.astype(BF16)
-    ex_cot = exchange(EX_COT, cb, 2, RIM, cb, 2, sec)
-    for copy in ex_cot:
-        copy.start()
+        cb[HALO_C + p, pl.ds(RIM, COLS), :] = jnp.concatenate(pieces, axis=0).T.astype(BF16)
+    ex_cot = exchange(EX_COT, cb, HALO_C)
+    start_all(ex_cot)
 
     col_at = iota((WIDE, PAIR), 0) - RIM + col * COLS
     col_mask[...] = one_hot((col_at >= 0) & (col_at < cols * COLS))
@@ -249,6 +288,51 @@
     pack_forward(lambda a, b: w_input_v[a, b].astype(F32), (k_feat, k_state))
     pack_forward(lambda a, b: w_middle_v[a, b].astype(F32), (k_middle,))
     pack_forward(lambda a, b: w_output_v[a, b].astype(F32), (k_output,))
+    ex_kernels = [
+        pltpu.make_async_remote_copy(
+            src_ref=mine,
+            dst_ref=theirs,
+            send_sem=send_sem.at[EX_KERNELS, k],
+            recv_sem=recv_sem.at[EX_KERNELS, k],
+            device_id=(other, row, col),
+            device_id_type=MESH,
+        )
+        for k, (mine, theirs) in enumerate(
+            ((k_feat, k_feat_o), (k_middle, k_middle_o), (k_output, k_output_o))
+        )
+    ]
+
+    @pl.when(sec == 0)
+    def _():
+        for copy in ex_kernels:
+            copy.start()
+
+    load_head.wait()
+    m_at, n_at = iota((64, 48), 0), iota((64, 48), 1)
+    order = one_hot((n_at == (m_at & 15) * 4 + (m_at >> 4)) & ((m_at & 15) < 12)).astype(BF16)
+    for a in range(3):
+        for b in range(3):
+            head_rows[a, b] = jnp.dot(order, w_head_v[a, b], preferred_element_type=F32)
+    pack_transposed(lambda a, b: head_rows[2 - a, 2 - b], k_head_t)
+    load_second.wait()
+    pack_transposed(lambda a, b: w_second_v[2 - a, 2 - b].astype(F32), k_second_t)
+
+    load_merge.wait()
+
+    @pl.when(sec == 0)
+    def _():
+        pack_forward(lambda a, b: w_merge_v[a, b].astype(F32), (k_merge2, k_merge1))
+
+    @pl.when(sec == 1)
+    def _():
+        pack_forward(lambda a, b: w_merge_v[a, b].astype(F32), (k_merge1, k_merge2))
+
+    load_first.wait()
+    pack_forward(lambda a, b: w_first_v[a, b].astype(F32), (k_first,))
+    pack_forward(lambda a, b: w_second_v[a, b].astype(F32), (k_second,))
+    pack_forward(lambda a, b: head_rows[a, b], (k_head,))
+    pack_transposed(lambda a, b: w_first_v[2 - a, 2 - b].astype(F32), k_first_t)
+    pack_transposed(lambda a, b: w_merge_v[2 - a, 2 - b].astype(F32), k_merge_t)
 
     def conv(sources, matrices, j):
         total = None
@@ -276,96 +360,59 @@
         )
         return pltpu.roll(mixed, 64, 1).astype(BF16)
 
-    for copy in ex_first:
-        copy.wait_recv()
-    clear_outside(xf1, 3)
+    receive_all(ex_first)
+    for j in range(13):
+        v = conv((xf1,), (k_feat,), j)
+        lift1[j] = (lrelu(v) * inside(2 * j - 9)).astype(BF16)
+    for j in range(12):
+        v = conv((lift1,), (k_middle,), j)
+        inner1[j] = (jnp.maximum(v, 0.0) * inside(2 * j - 8)).astype(BF16)
+    for j in range(11):
+        v = conv((inner1,), (k_output,), j) + lift1[j + 1].astype(F32)
+        state1[j] = (v * inside(2 * j - 7)).astype(BF16)
+
+    @pl.when(sec == 1)
+    def _():
+        for copy in ex_kernels:
+            copy.wait_recv()
+        for copy in ex_kernels:
+            copy.start()
+
+    receive_all(ex_second)
+    for j in range(11):
+        xo2[j] = realign(xf2[j], xf2[j + 1])
+    for j in range(10):
+        v = conv((xo2, state1), (k_feat, k_state), j)
+        lift2[j] = (lrelu(v) * inside(2 * j - 6)).astype(BF16)
     for j in range(9):
-        v = conv((xf1,), (k_feat,), j)
-        lift1[j] = (lrelu(v) * inside(2 * j - 5)).astype(BF16)
+        v = conv((lift2,), (k_middle,), j)
+        inner2[j] = (jnp.maximum(v, 0.0) * inside(2 * j - 5)).astype(BF16)
     for j in range(8):
-        v = conv((lift1,), (k_middle,), j)
-        inner1[j] = (jnp.maximum(v, 0.0) * inside(2 * j - 4)).astype(BF16)
-    for j in range(7):
-        v = conv((inner1,), (k_output,), j) + lift1[j + 1].astype(F32)
-        state1[j] = (v * inside(2 * j - 3)).astype(BF16)
-    for p in range(OWN):
-        e1[p] = realign(
-            state1[p + 1, pl.ds(RIM, COLS), :], state1[p + 2, pl.ds(RIM, COLS), :]
-        )
-    ex_state1 = exchange(EX_STATE1, e1, 0, 0, s1, 2, other)
-    ex_state1.append(
-        pltpu.make_async_remote_copy(
-            src_ref=e1,
-            dst_ref=s1.at[pl.ds(2, OWN), pl.ds(RIM, COLS), :],
-            send_sem=send_sem.at[EX_STATE1, 8],
-            recv_sem=recv_sem.at[EX_STATE1, 8],
-            device_id=(other, row, col),
-            device_id_type=MESH,
-        )
-    )
-    for copy in ex_state1:
-        copy.start()
-
-    for copy in ex_second:
-        copy.wait_recv()
-    clear_outside(xf2, 2)
-    for j in range(7):
-        xo2[j] = realign(xf2[j], xf2[j + 1])
-    for j in range(6):
-        v = conv((xo2, state1), (k_feat, k_state), j)
-        lift2[j] = (lrelu(v) * inside(2 * j - 2)).astype(BF16)
-    for j in range(5):
-        v = conv((lift2,), (k_middle,), j)
-        inner2[j] = (jnp.maximum(v, 0.0) * inside(2 * j - 1)).astype(BF16)
-    for j in range(4):
         v = conv((inner2,), (k_output,), j) + lift2[j + 1].astype(F32)
-        s2[2 + j, pl.ds(RIM, COLS), :] = v[RIM : RIM + COLS].astype(BF16)
-    ex_state2 = exchange(EX_STATE2, s2, 2, RIM, s2, 2, sec)
-    for copy in ex_state2:
-        copy.start()
-
-    load_head.wait()
-    m_at, n_at = iota((64, 48), 0), iota((64, 48), 1)
-    order = one_hot((n_at == (m_at & 15) * 4 + (m_at >> 4)) & ((m_at & 15) < 12)).astype(BF16)
-    for a in range(3):
-        for b in range(3):
-            head_rows[a, b] = jnp.dot(order, w_head_v[a, b], preferred_element_type=F32)
-    pack_transposed(lambda a, b: head_rows[2 - a, 2 - b], k_head_t)
-    load_second.wait()
-    pack_transposed(lambda a, b: w_second_v[2 - a, 2 - b].astype(F32), k_second_t)
-
-    for copy in ex_cot:
-        copy.wait_recv()
-    clear_outside(cb, 2)
+        s2[j] = (v * inside(2 * j - 4)).astype(BF16)
+
+    receive_all(ex_cot)
     for j in range(7):
         v = conv((cb,), (k_head_t,), j)
         grad_ref[j] = (v * inside(2 * j - 3)).astype(BF16)
     for j in range(6):
         grad_in_pre[j] = conv((grad_ref,), (k_second_t,), j) * inside(2 * j - 2)
 
-    load_merge.wait()
-
     @pl.when(sec == 0)
     def _():
-        pack_forward(lambda a, b: w_merge_v[a, b].astype(F32), (k_merge2, k_merge1))
-
-    @pl.when(sec == 1)
-    def _():
-        pack_forward(lambda a, b: w_merge_v[a, b].astype(F32), (k_merge1, k_merge2))
-
-    load_first.wait()
-    pack_forward(lambda a, b: w_first_v[a, b].astype(F32), (k_first,))
-    pack_forward(lambda a, b: w_second_v[a, b].astype(F32), (k_second,))
-    pack_forward(lambda a, b: head_rows[a, b], (k_head,))
-    pack_transposed(lambda a, b: w_first_v[2 - a, 2 - b].astype(F32), k_first_t)
-    pack_transposed(lambda a, b: w_merge_v[2 - a, 2 - b].astype(F32), k_merge_t)
-
-    for copy in ex_state1:
-        copy.wait_recv()
-    clear_outside(s1, 2)
-    for copy in ex_state2:
-        copy.wait_recv()
-    clear_outside(s2, 2)
+        for copy in ex_kernels:
+            copy.wait_recv()
+
+    for j in range(10):
+        v = conv((xo2,), (k_feat_o,), j)
+        lift3[j] = (lrelu(v) * inside(2 * j - 6)).astype(BF16)
+    for j in range(9):
+        v = conv((lift3,), (k_middle_o,), j)
+        inner3[j] = (jnp.maximum(v, 0.0) * inside(2 * j - 5)).astype(BF16)
+    for j in range(8):
+        v = conv((inner3,), (k_output_o,), j) + lift3[j + 1].astype(F32)
+        s1[j] = (v * inside(2 * j - 4)).astype(BF16)
+
     for j in range(7):
         v = conv((s1, s2), (k_merge1, k_merge2), j)
         sigma = jax.nn.sigmoid(v)
@@ -415,9 +462,10 @@
     store_adj = pltpu.make_async_copy(adj_v, adj_out, store_sem.at[1])
     store_adj.start()
 
-    for copies in (ex_first, ex_second, ex_cot, ex_state1, ex_state2):
-        for copy in copies:
-            copy.wait_send()
+    for copies in (ex_first, ex_second, ex_cot):
+        sent_all(copies)
+    for copy in ex_kernels:
+        copy.wait_send()
     store_up.wait()
     store_adj.wait()
 
@@ -456,18 +504,19 @@
             vmem(3, 3, 48, 64),
             vmem(96, 512),
             vmem(512, 128, dtype=F32),
-            act(10),
-            act(8),
-            act(7),
+            act(OWN + 2 * HALO_A),
+            act(OWN + 2 * HALO_B),
+            act(11),
+            act(OWN + 2 * HALO_C),
             act(8),
             act(8),
-            act(8),
-            vmem(OWN, COLS, PAIR),
+            act(13),
+            act(12),
+            act(11),
+            act(10),
             act(9),
-            act(8),
-            act(7),
-            act(6),
-            act(5),
+            act(10),
+            act(9),
             act(7),
             act(5, F32),
             act(6),
@@ -477,7 +526,7 @@
             act(6),
             act(5),
         ]
-        + [vmem(256, 384) for _ in range(12)]
+        + [vmem(256, 384) for _ in range(15)]
         + [
             vmem(256, 768),
             vmem(3, 3, 64, 64, dtype=F32),
@@ -489,8 +538,8 @@
             vmem(WIDE, PAIR, dtype=F32),
             pltpu.SemaphoreType.DMA((10,)),
             pltpu.SemaphoreType.DMA((2,)),
-            pltpu.SemaphoreType.DMA((5, 9)),
-            pltpu.SemaphoreType.DMA((5, 9)),
+            pltpu.SemaphoreType.DMA((4, len(AROUND))),
+            pltpu.SemaphoreType.DMA((4, len(AROUND))),
         ]
     )
     up, adj = pl.pallas_call(
@@ -503,7 +552,7 @@
         out_specs=(pl.BlockSpec(memory_space=pl.ANY), pl.BlockSpec(memory_space=pl.ANY)),
         scratch_shapes=scratch,
         compiler_params=pltpu.CompilerParams(
-            collective_id=0, has_side_effects=True, vmem_limit_bytes=48 * 1024 * 1024
+            collective_id=0, has_side_effects=True, vmem_limit_bytes=60 * 1024 * 1024
         ),
     )(
         features.reshape(2, 512, 128),

time: 46.1 us -> 30.5 us (0.66)
  the two profiles are of different devices: /device:TPU:1 before, /device:TPU:104 now
where the time goes in v1:
time: 30.5 us; the launch traced here: 30.3 us
  Pallas kernels  26.1 us (86%)
  local copies, waits for them, and re-layouts  3.48 us (11%)
  between operations  0.64 us (2%)
    pallas_call x1, Pallas kernels, on_device(): pl.pallas_call(functools.partial(kernel, rows, cols), out_shape=(jax.Shap...  26.1 us
    unnamed x2, local copies, waits for them, and re-layouts  3.48 us

profile of v1, /device:TPU:104, one launch (start us, length us, event | category | flops | bytes accessed | tf_op | source)
XLA Modules:
  0.0 30.3 jit_solution(8224376062433911649)
XLA Ops:
  0.6 26.1 %shard_map.104 = (f32[96,512]{1,0:T(8,128)}, f32[1024,128]{1,0:T(8,128)}) custom-call(bf16[2,512,128]{2,1,0:T(8,128)(2,1)} %bitcast.18, bf16[3,3,64,128]{3,2,1,0:T(8,128)(2,1)} %bitcast.20, bf16[3,3,64,64]{3,2,1,0:T(8,128)(2,1)} %bitcast.21, bf16[3,3,64,64]{3,2,1,0:T(8,128)(2,1)} %bitcast.22, bf16[3,3,64,128]{3,2,1,0:T(8,128)(2,1)} %bitcast.23, ...), custom_call_target="tpu_custom_call" | custom-call | tf_op jit(solution)/shard_map/pallas_call | solution.py:545
  26.8 1.6 %copy.13 = f32[1,3,32,512]{3,2,1,0:T(8,128)} copy(f32[1,3,32,512]{3,2,1,0:T(8,128)} %bitcast.19) | data formatting | bytes 393216
  28.4 1.9 %copy.14 = f32[1,128,8,128]{3,2,1,0:T(8,128)} copy(f32[1,128,8,128]{3,2,1,0:T(8,128)} %bitcast.17) | data formatting | bytes 1048576

commit v2 on v1

--- a/solution.py
+++ b/solution.py
@@ -24,7 +24,7 @@
     (dr, dc) for dr in (-1, 1, 0, -2, 2) for dc in (0, -1, 1) if (dr, dc) != (0, 0)
 )
 
-EX_FIRST, EX_SECOND, EX_COT, EX_KERNELS = range(4)
+EX_FIRST, EX_SECOND, EX_COT, EX_STATE = range(4)
 
 
 def iota(shape, dim):
@@ -74,8 +74,7 @@
     state1,
     lift2,
     inner2,
-    lift3,
-    inner3,
+    e1,
     merged,
     slope_m,
     rec_inner,
@@ -88,9 +87,6 @@
     k_state,
     k_middle,
     k_output,
-    k_feat_o,
-    k_middle_o,
-    k_output_o,
     k_merge2,
     k_merge1,
     k_first,
@@ -155,13 +151,10 @@
         def _(dr=dr, dc=dc):
             pl.semaphore_signal(barrier, inc=1, device_id=place(dr, dc), device_id_type=MESH)
 
-    @pl.when(sec == 1)
-    def _():
-        pl.semaphore_signal(barrier, inc=1, device_id=(other, row, col), device_id_type=MESH)
-
+    pl.semaphore_signal(barrier, inc=1, device_id=(other, row, col), device_id_type=MESH)
     near_rows = jnp.minimum(row + REACH, rows - 1) - jnp.maximum(row - REACH, 0) + 1
     near_cols = jnp.minimum(col + 1, cols - 1) - jnp.maximum(col - 1, 0) + 1
-    greetings = near_rows * near_cols - sec
+    greetings = near_rows * near_cols
 
     def exchange(kind, buf, halo):
         copies = []
@@ -199,7 +192,7 @@
         for copy, to, _ in copies:
             pl.when(to)(copy.wait_send)
 
-    halos = ((xf1, HALO_A), (xf2, HALO_B), (cb, HALO_C))
+    halos = ((xf1, HALO_A), (cb, HALO_C))
 
     def clear_rows(up, tiles):
         for buf, halo in halos:
@@ -233,8 +226,36 @@
     start_all(ex_first)
     load_f2.wait()
     turn_features(1, xf2, HALO_B)
-    ex_second = exchange(EX_SECOND, xf2, HALO_B)
-    start_all(ex_second)
+
+    def pass_on(kind, parts):
+        return [
+            pltpu.make_async_remote_copy(
+                src_ref=src,
+                dst_ref=dst,
+                send_sem=send_sem.at[kind, k],
+                recv_sem=recv_sem.at[kind, k],
+                device_id=(other, row, col),
+                device_id_type=MESH,
+            )
+            for k, (src, dst) in enumerate(parts)
+        ]
+
+    def same(at, n, start, width):
+        return tuple(
+            buf.at[pl.ds(halo + at, n), pl.ds(start, width), :]
+            for buf, halo in ((xf1, HALO_A), (xf2, HALO_B))
+        )
+
+    ex_second = pass_on(
+        EX_SECOND,
+        (
+            same(-HALO_B, HALO_B, 0, WIDE),
+            same(OWN, HALO_B, 0, WIDE),
+            same(0, OWN, 0, RIM),
+            same(0, OWN, RIM + COLS, RIM),
+        ),
+    )
+    ex_state = pass_on(EX_STATE, ((e1, s1),))
 
     k_at, n_at = iota((512, 512), 0), iota((512, 512), 1)
     shuffle[...] = one_hot(n_at == 4 * (k_at & 127) + (k_at >> 7)).astype(BF16)
@@ -288,24 +309,6 @@
     pack_forward(lambda a, b: w_input_v[a, b].astype(F32), (k_feat, k_state))
     pack_forward(lambda a, b: w_middle_v[a, b].astype(F32), (k_middle,))
     pack_forward(lambda a, b: w_output_v[a, b].astype(F32), (k_output,))
-    ex_kernels = [
-        pltpu.make_async_remote_copy(
-            src_ref=mine,
-            dst_ref=theirs,
-            send_sem=send_sem.at[EX_KERNELS, k],
-            recv_sem=recv_sem.at[EX_KERNELS, k],
-            device_id=(other, row, col),
-            device_id_type=MESH,
-        )
-        for k, (mine, theirs) in enumerate(
-            ((k_feat, k_feat_o), (k_middle, k_middle_o), (k_output, k_output_o))
-        )
-    ]
-
-    @pl.when(sec == 0)
-    def _():
-        for copy in ex_kernels:
-            copy.start()
 
     load_head.wait()
     m_at, n_at = iota((64, 48), 0), iota((64, 48), 1)
@@ -361,6 +364,8 @@
         return pltpu.roll(mixed, 64, 1).astype(BF16)
 
     receive_all(ex_first)
+    for copy in ex_second:
+        copy.start()
     for j in range(13):
         v = conv((xf1,), (k_feat,), j)
         lift1[j] = (lrelu(v) * inside(2 * j - 9)).astype(BF16)
@@ -371,14 +376,13 @@
         v = conv((inner1,), (k_output,), j) + lift1[j + 1].astype(F32)
         state1[j] = (v * inside(2 * j - 7)).astype(BF16)
 
-    @pl.when(sec == 1)
-    def _():
-        for copy in ex_kernels:
-            copy.wait_recv()
-        for copy in ex_kernels:
-            copy.start()
-
-    receive_all(ex_second)
+    for m in range(8):
+        e1[m] = realign(state1[m + 1], state1[m + 2])
+    for copy in ex_state:
+        copy.start()
+
+    for copy in ex_second:
+        copy.wait_recv()
     for j in range(11):
         xo2[j] = realign(xf2[j], xf2[j + 1])
     for j in range(10):
@@ -398,21 +402,8 @@
     for j in range(6):
         grad_in_pre[j] = conv((grad_ref,), (k_second_t,), j) * inside(2 * j - 2)
 
-    @pl.when(sec == 0)
-    def _():
-        for copy in ex_kernels:
-            copy.wait_recv()
-
-    for j in range(10):
-        v = conv((xo2,), (k_feat_o,), j)
-        lift3[j] = (lrelu(v) * inside(2 * j - 6)).astype(BF16)
-    for j in range(9):
-        v = conv((lift3,), (k_middle_o,), j)
-        inner3[j] = (jnp.maximum(v, 0.0) * inside(2 * j - 5)).astype(BF16)
-    for j in range(8):
-        v = conv((inner3,), (k_output_o,), j) + lift3[j + 1].astype(F32)
-        s1[j] = (v * inside(2 * j - 4)).astype(BF16)
-
+    for copy in ex_state:
+        copy.wait_recv()
     for j in range(7):
         v = conv((s1, s2), (k_merge1, k_merge2), j)
         sigma = jax.nn.sigmoid(v)
@@ -462,12 +453,23 @@
     store_adj = pltpu.make_async_copy(adj_v, adj_out, store_sem.at[1])
     store_adj.start()
 
-    for copies in (ex_first, ex_second, ex_cot):
+    for copies in (ex_first, ex_cot):
         sent_all(copies)
-    for copy in ex_kernels:
+    for copy in ex_second + ex_state:
         copy.wait_send()
     store_up.wait()
     store_adj.wait()
+
+
+def hand_over(up_in, adj_in, up_out, adj_out, sem):
+    copies = [pltpu.make_async_copy(up_in, up_out, sem.at[0])]
+    for k in range(4):
+        part = pl.ds(k * 256, 256)
+        copies.append(pltpu.make_async_copy(adj_in.at[part], adj_out.at[part], sem.at[1 + k]))
+    for copy in copies:
+        copy.start()
+    for copy in copies:
+        copy.wait()
 
 
 def on_device(
@@ -515,8 +517,7 @@
             act(11),
             act(10),
             act(9),
-            act(10),
-            act(9),
+            act(8),
             act(7),
             act(5, F32),
             act(6),
@@ -526,7 +527,7 @@
             act(6),
             act(5),
         ]
-        + [vmem(256, 384) for _ in range(15)]
+        + [vmem(256, 384) for _ in range(12)]
         + [
             vmem(256, 768),
             vmem(3, 3, 64, 64, dtype=F32),
@@ -565,6 +566,16 @@
         taps(head_weight),
         cotangent.reshape(96, 512),
     )
+    up, adj = pl.pallas_call(
+        hand_over,
+        out_shape=(
+            jax.ShapeDtypeStruct((96, 512), F32),
+            jax.ShapeDtypeStruct((1024, 128), F32),
+        ),
+        in_specs=[pl.BlockSpec(memory_space=pl.ANY)] * 2,
+        out_specs=(pl.BlockSpec(memory_space=pl.ANY), pl.BlockSpec(memory_space=pl.ANY)),
+        scratch_shapes=[pltpu.SemaphoreType.DMA((5,))],
+    )(up, adj)
     return up.reshape(1, 3, 32, 512), adj.reshape(1, 128, 8, 128)
 
 

time: 30.5 us -> 47.1 us (1.54)
  the two profiles are of different devices: /device:TPU:104 before, /device:TPU:1 now
where the time goes in v2:
time: 47.1 us; the launch traced here: 46.6 us
  Pallas kernels  45.9 us (97%)
  between operations  0.64 us (1%)
    pallas_call x1, Pallas kernels, on_device(): pl.pallas_call(hand_over, out_shape=(jax.ShapeDtypeStruct((96, 512), F32)...  23 us
    pallas_call x1, Pallas kernels, on_device(): pl.pallas_call(functools.partial(kernel, rows, cols), out_shape=(jax.Shap...  22.9 us

profile of v2, /device:TPU:1, one launch (start us, length us, event | category | flops | bytes accessed | tf_op | source)
XLA Modules:
  0.0 46.6 jit_solution(7286883537131538045)
XLA Ops:
  0.6 22.9 %shard_map.104 = (f32[96,512]{1,0:T(8,128)}, f32[1024,128]{1,0:T(8,128)}) custom-call(bf16[2,512,128]{2,1,0:T(8,128)(2,1)} %bitcast.17, bf16[3,3,64,128]{3,2,1,0:T(8,128)(2,1)} %bitcast.18, bf16[3,3,64,64]{3,2,1,0:T(8,128)(2,1)} %bitcast.19, bf16[3,3,64,64]{3,2,1,0:T(8,128)(2,1)} %bitcast.20, bf16[3,3,64,128]{3,2,1,0:T(8,128)(2,1)} %bitcast.21, ...), custom_call_target="tpu_custom_call" | custom-call | tf_op jit(solution)/shard_map/pallas_call | solution.py:546
  23.6 23.0 %shard_map.105 = (f32[96,512]{1,0:T(8,128)}, f32[1024,128]{1,0:T(8,128)}) custom-call(f32[96,512]{1,0:T(8,128)} %get-tuple-element.6.up_in, f32[1024,128]{1,0:T(8,128)} %get-tuple-element.7.adj_in), custom_call_target="tpu_custom_call" | custom-call | tf_op jit(solution)/shard_map/pallas_call | solution.py:569

commit v3 on v2

--- a/solution.py
+++ b/solution.py
@@ -21,7 +21,10 @@
 REACH = 2
 
 AROUND = tuple(
-    (dr, dc) for dr in (-1, 1, 0, -2, 2) for dc in (0, -1, 1) if (dr, dc) != (0, 0)
+    (dr, dc)
+    for dc in (0, -1, 1)
+    for dr in (-1, 1, 0, -2, 2)
+    if (dr, dc) != (0, 0)
 )
 
 EX_FIRST, EX_SECOND, EX_COT, EX_STATE = range(4)
@@ -83,12 +86,10 @@
     grad_in_pre,
     grad_in,
     grad_pre,
-    k_feat,
-    k_state,
+    k_prop,
     k_middle,
     k_output,
-    k_merge2,
-    k_merge1,
+    k_merge,
     k_first,
     k_second,
     k_head,
@@ -100,11 +101,8 @@
     shuffle,
     z_hi,
     z_lo,
-    up_v,
-    adj_v,
     col_mask,
     load_sem,
-    store_sem,
     send_sem,
     recv_sem,
 ):
@@ -124,6 +122,27 @@
         return copy
 
     load_f1 = load(feat.at[first_frame], feat_v.at[0])
+
+    barrier = pltpu.get_barrier_semaphore()
+
+    def exists(dr, dc):
+        there = None
+        for at, size, d in ((row, rows, dr), (col, cols, dc)):
+            if d != 0:
+                ok = at + d < size if d > 0 else at + d >= 0
+                there = ok if there is None else there & ok
+        return there
+
+    def place(dr, dc):
+        return (sec, lax.rem(row + dr + rows, rows), lax.rem(col + dc + cols, cols))
+
+    for dr, dc in AROUND:
+
+        @pl.when(exists(dr, dc))
+        def _(dr=dr, dc=dc):
+            pl.semaphore_signal(barrier, inc=1, device_id=place(dr, dc), device_id_type=MESH)
+
+    pl.semaphore_signal(barrier, inc=1, device_id=(other, row, col), device_id_type=MESH)
     load_f2 = load(feat.at[second_frame], feat_v.at[1])
     load_cot = load(cot, cot_v)
     load_prop = [load(w_input, w_input_v), load(w_middle, w_middle_v), load(w_output, w_output_v)]
@@ -132,26 +151,6 @@
     load_merge = load(w_merge, w_merge_v)
     load_first = load(w_first, w_first_v)
 
-    barrier = pltpu.get_barrier_semaphore()
-
-    def exists(dr, dc):
-        there = None
-        for at, size, d in ((row, rows, dr), (col, cols, dc)):
-            if d != 0:
-                ok = at + d < size if d > 0 else at + d >= 0
-                there = ok if there is None else there & ok
-        return there
-
-    def place(dr, dc):
-        return (sec, lax.rem(row + dr + rows, rows), lax.rem(col + dc + cols, cols))
-
-    for dr, dc in AROUND:
-
-        @pl.when(exists(dr, dc))
-        def _(dr=dr, dc=dc):
-            pl.semaphore_signal(barrier, inc=1, device_id=place(dr, dc), device_id_type=MESH)
-
-    pl.semaphore_signal(barrier, inc=1, device_id=(other, row, col), device_id_type=MESH)
     near_rows = jnp.minimum(row + REACH, rows - 1) - jnp.maximum(row - REACH, 0) + 1
     near_cols = jnp.minimum(col + 1, cols - 1) - jnp.maximum(col - 1, 0) + 1
     greetings = near_rows * near_cols
@@ -177,19 +176,20 @@
                 device_id=place(dr, dc),
                 device_id_type=MESH,
             )
-            copies.append((copy, exists(dr, dc), exists(-dr, -dc)))
+            copies.append((copy, exists(dr, dc), exists(-dr, -dc), dr))
         return copies
 
     def start_all(copies):
-        for copy, to, _ in copies:
+        for copy, to, _, _ in copies:
             pl.when(to)(copy.start)
 
-    def receive_all(copies):
-        for copy, _, source in copies:
-            pl.when(source)(copy.wait_recv)
+    def receive_all(copies, tiles=(0, 1, 2)):
+        for copy, _, source, dr in copies:
+            if abs(dr) in tiles:
+                pl.when(source)(copy.wait_recv)
 
     def sent_all(copies):
-        for copy, to, _ in copies:
+        for copy, to, _, _ in copies:
             pl.when(to)(copy.wait_send)
 
     halos = ((xf1, HALO_A), (cb, HALO_C))
@@ -306,7 +306,7 @@
 
     for copy in load_prop:
         copy.wait()
-    pack_forward(lambda a, b: w_input_v[a, b].astype(F32), (k_feat, k_state))
+    pack_forward(lambda a, b: w_input_v[a, b].astype(F32), (k_prop.at[pl.ds(0, 256)], k_prop.at[pl.ds(256, 256)]))
     pack_forward(lambda a, b: w_middle_v[a, b].astype(F32), (k_middle,))
     pack_forward(lambda a, b: w_output_v[a, b].astype(F32), (k_output,))
 
@@ -324,11 +324,11 @@
 
     @pl.when(sec == 0)
     def _():
-        pack_forward(lambda a, b: w_merge_v[a, b].astype(F32), (k_merge2, k_merge1))
+        pack_forward(lambda a, b: w_merge_v[a, b].astype(F32), (k_merge.at[pl.ds(256, 256)], k_merge.at[pl.ds(0, 256)]))
 
     @pl.when(sec == 1)
     def _():
-        pack_forward(lambda a, b: w_merge_v[a, b].astype(F32), (k_merge1, k_merge2))
+        pack_forward(lambda a, b: w_merge_v[a, b].astype(F32), (k_merge.at[pl.ds(0, 256)], k_merge.at[pl.ds(256, 256)]))
 
     load_first.wait()
     pack_forward(lambda a, b: w_first_v[a, b].astype(F32), (k_first,))
@@ -337,12 +337,9 @@
     pack_transposed(lambda a, b: w_first_v[2 - a, 2 - b].astype(F32), k_first_t)
     pack_transposed(lambda a, b: w_merge_v[2 - a, 2 - b].astype(F32), k_merge_t)
 
-    def conv(sources, matrices, j):
-        total = None
-        for source, matrix in zip(sources, matrices):
-            x = jnp.concatenate([source[j], source[j + 1]], axis=1)
-            y = jnp.dot(x, matrix[...], preferred_element_type=F32)
-            total = y if total is None else total + y
+    def conv(sources, matrix, j):
+        x = jnp.concatenate([s[j + k] for s in sources for k in range(2)], axis=1)
+        total = jnp.dot(x, matrix[...], preferred_element_type=F32)
         w = total.shape[1] // 3
         return (
             total[:, w : 2 * w]
@@ -363,17 +360,24 @@
         )
         return pltpu.roll(mixed, 64, 1).astype(BF16)
 
-    receive_all(ex_first)
+    def lift_first(at):
+        for j in at:
+            v = conv((xf1,), k_prop.at[pl.ds(0, 256)], j)
+            lift1[j] = (lrelu(v) * inside(2 * j - 9)).astype(BF16)
+
+    receive_all(ex_first, (0,))
+    lift_first(range(HALO_A, HALO_A + OWN - 1))
+    receive_all(ex_first, (1,))
     for copy in ex_second:
         copy.start()
-    for j in range(13):
-        v = conv((xf1,), (k_feat,), j)
-        lift1[j] = (lrelu(v) * inside(2 * j - 9)).astype(BF16)
+    lift_first((1, 2, 3, 4, 8, 9, 10, 11))
+    receive_all(ex_first, (2,))
+    lift_first((0, 12))
     for j in range(12):
-        v = conv((lift1,), (k_middle,), j)
+        v = conv((lift1,), k_middle, j)
         inner1[j] = (jnp.maximum(v, 0.0) * inside(2 * j - 8)).astype(BF16)
     for j in range(11):
-        v = conv((inner1,), (k_output,), j) + lift1[j + 1].astype(F32)
+        v = conv((inner1,), k_output, j) + lift1[j + 1].astype(F32)
         state1[j] = (v * inside(2 * j - 7)).astype(BF16)
 
     for m in range(8):
@@ -386,40 +390,40 @@
     for j in range(11):
         xo2[j] = realign(xf2[j], xf2[j + 1])
     for j in range(10):
-        v = conv((xo2, state1), (k_feat, k_state), j)
+        v = conv((xo2, state1), k_prop, j)
         lift2[j] = (lrelu(v) * inside(2 * j - 6)).astype(BF16)
     for j in range(9):
-        v = conv((lift2,), (k_middle,), j)
+        v = conv((lift2,), k_middle, j)
         inner2[j] = (jnp.maximum(v, 0.0) * inside(2 * j - 5)).astype(BF16)
     for j in range(8):
-        v = conv((inner2,), (k_output,), j) + lift2[j + 1].astype(F32)
+        v = conv((inner2,), k_output, j) + lift2[j + 1].astype(F32)
         s2[j] = (v * inside(2 * j - 4)).astype(BF16)
 
     receive_all(ex_cot)
     for j in range(7):
-        v = conv((cb,), (k_head_t,), j)
+        v = conv((cb,), k_head_t, j)
         grad_ref[j] = (v * inside(2 * j - 3)).astype(BF16)
     for j in range(6):
-        grad_in_pre[j] = conv((grad_ref,), (k_second_t,), j) * inside(2 * j - 2)
+        grad_in_pre[j] = conv((grad_ref,), k_second_t, j) * inside(2 * j - 2)
 
     for copy in ex_state:
         copy.wait_recv()
     for j in range(7):
-        v = conv((s1, s2), (k_merge1, k_merge2), j)
+        v = conv((s1, s2), k_merge, j)
         sigma = jax.nn.sigmoid(v)
         merged[j] = (v * sigma * inside(2 * j - 3)).astype(BF16)
         if 1 <= j <= 5:
             slope_m[j - 1] = sigma * (1.0 + v * (1.0 - sigma)) * inside(2 * j - 3)
     for j in range(6):
-        v = conv((merged,), (k_first,), j)
+        v = conv((merged,), k_first, j)
         sigma = jax.nn.sigmoid(v)
         rec_inner[j] = (v * sigma * inside(2 * j - 2)).astype(BF16)
         grad_in[j] = (grad_in_pre[j] * (sigma * (1.0 + v * (1.0 - sigma)))).astype(BF16)
     for j in range(5):
-        v = conv((rec_inner,), (k_second,), j) + merged[j + 1].astype(F32)
+        v = conv((rec_inner,), k_second, j) + merged[j + 1].astype(F32)
         refined[j] = (v * inside(2 * j - 1)).astype(BF16)
     for j in range(4):
-        v = conv((refined,), (k_head,), j)[RIM : RIM + COLS].T
+        v = conv((refined,), k_head, j)[RIM : RIM + COLS].T
         high = v.astype(BF16)
         low = (v - high.astype(F32)).astype(BF16)
         for r in range(2):
@@ -437,28 +441,22 @@
         ordered = jnp.dot(gather, z[...], preferred_element_type=F32).astype(BF16)
         part = jnp.dot(ordered, shuffle[...], preferred_element_type=F32)
         total = part if total is None else total + part
-    up_v[...] = total
-    store_up = pltpu.make_async_copy(up_v, up_out, store_sem.at[0])
-    store_up.start()
+    up_out[...] = total
 
     for j in range(5):
-        v = conv((grad_in,), (k_first_t,), j) + grad_ref[j + 1].astype(F32)
+        v = conv((grad_in,), k_first_t, j) + grad_ref[j + 1].astype(F32)
         grad_pre[j] = (v * slope_m[j]).astype(BF16)
     for j in range(4):
-        v = conv((grad_pre,), (k_merge_t,), j)
+        v = conv((grad_pre,), k_merge_t, j)
         for r in range(2):
-            adj_v[pl.ds(2 * j + r, 128, stride=8), :] = v[
+            adj_out[pl.ds(2 * j + r, 128, stride=8), :] = v[
                 RIM : RIM + COLS, r * 128 : (r + 1) * 128
             ].T
-    store_adj = pltpu.make_async_copy(adj_v, adj_out, store_sem.at[1])
-    store_adj.start()
 
     for copies in (ex_first, ex_cot):
         sent_all(copies)
     for copy in ex_second + ex_state:
         copy.wait_send()
-    store_up.wait()
-    store_adj.wait()
 
 
 def hand_over(up_in, adj_in, up_out, adj_out, sem):
@@ -527,30 +525,28 @@
             act(6),
             act(5),
         ]
-        + [vmem(256, 384) for _ in range(12)]
+        + [vmem(512, 384), vmem(256, 384), vmem(256, 384), vmem(512, 384)]
+        + [vmem(256, 384) for _ in range(6)]
         + [
             vmem(256, 768),
             vmem(3, 3, 64, 64, dtype=F32),
             vmem(512, 512),
             vmem(128, 512),
             vmem(128, 512),
-            vmem(96, 512, dtype=F32),
-            vmem(1024, 128, dtype=F32),
             vmem(WIDE, PAIR, dtype=F32),
             pltpu.SemaphoreType.DMA((10,)),
-            pltpu.SemaphoreType.DMA((2,)),
             pltpu.SemaphoreType.DMA((4, len(AROUND))),
             pltpu.SemaphoreType.DMA((4, len(AROUND))),
         ]
     )
     up, adj = pl.pallas_call(
         functools.partial(kernel, rows, cols),
-        out_shape=(
-            jax.ShapeDtypeStruct((96, 512), F32),
-            jax.ShapeDtypeStruct((1024, 128), F32),
+        out_shape=(pltpu.VMEM((96, 512), F32), pltpu.VMEM((1024, 128), F32)),
+        in_specs=[pl.BlockSpec(memory_space=pl.ANY)] * 9,
+        out_specs=(
+            pl.BlockSpec(memory_space=pltpu.VMEM),
+            pl.BlockSpec(memory_space=pltpu.VMEM),
         ),
-        in_specs=[pl.BlockSpec(memory_space=pl.ANY)] * 9,
-        out_specs=(pl.BlockSpec(memory_space=pl.ANY), pl.BlockSpec(memory_space=pl.ANY)),
         scratch_shapes=scratch,
         compiler_params=pltpu.CompilerParams(
             collective_id=0, has_side_effects=True, vmem_limit_bytes=60 * 1024 * 1024
@@ -572,10 +568,10 @@
             jax.ShapeDtypeStruct((96, 512), F32),
             jax.ShapeDtypeStruct((1024, 128), F32),
         ),
-        in_specs=[pl.BlockSpec(memory_space=pl.ANY)] * 2,
+        in_specs=[pl.BlockSpec(memory_space=pltpu.VMEM)] * 2,
         out_specs=(pl.BlockSpec(memory_space=pl.ANY), pl.BlockSpec(memory_space=pl.ANY)),
         scratch_shapes=[pltpu.SemaphoreType.DMA((5,))],
-    )(up, adj)
+    )(*(pltpu.with_memory_space_constraint(a, pltpu.VMEM) for a in (up, adj)))
     return up.reshape(1, 3, 32, 512), adj.reshape(1, 128, 8, 128)
 
 

time: 47.1 us -> 24.3 us (0.52)
  the two profiles are of different devices: /device:TPU:1 before, /device:TPU:120 now
where the time goes in v3:
time: 24.3 us; the launch traced here: 24.2 us
  Pallas kernels  23.6 us (97%)
  between operations  0.64 us (3%)
    pallas_call x1, Pallas kernels, on_device(): pl.pallas_call(functools.partial(kernel, rows, cols), out_shape=(pltpu.VM...  22.7 us
    pallas_call x1, Pallas kernels, on_device(): pl.pallas_call(hand_over, out_shape=(jax.ShapeDtypeStruct((96, 512), F32)...  0.89 us

profile of v3, /device:TPU:120, one launch (start us, length us, event | category | flops | bytes accessed | tf_op | source)
XLA Modules:
  0.0 24.2 jit_solution(2551135035084670197)
XLA Ops:
  0.6 22.7 %shard_map.104 = (f32[96,512]{1,0:T(8,128)S(1)}, f32[1024,128]{1,0:T(8,128)S(1)}) custom-call(bf16[2,512,128]{2,1,0:T(8,128)(2,1)} %bitcast.17, bf16[3,3,64,128]{3,2,1,0:T(8,128)(2,1)} %bitcast.18, bf16[3,3,64,64]{3,2,1,0:T(8,128)(2,1)} %bitcast.19, bf16[3,3,64,64]{3,2,1,0:T(8,128)(2,1)} %bitcast.20, bf16[3,3,64,128]{3,2,1,0:T(8,128)(2,1)} %bitcast.21, ...), custom_call_target="tpu_custom_call" | custom-call | tf_op jit(solution)/shard_map/pallas_call | solution.py:542
  23.3 0.9 %shard_map.105 = (f32[96,512]{1,0:T(8,128)}, f32[1024,128]{1,0:T(8,128)}) custom-call(f32[96,512]{1,0:T(8,128)S(1)} %get-tuple-element.6.up_in, f32[1024,128]{1,0:T(8,128)S(1)} %get-tuple-element.7.adj_in), custom_call_target="tpu_custom_call" | custom-call | tf_op jit(solution)/shard_map/pallas_call | solution.py:565
